TPU v7x, 128 devices: a whole 4x4x4 slice. The times are simulated.
128 devices in a mesh: gx: 8 (over x, z_lo), gy: 16 (over z_hi, y, core).
Axes of the slice: x: 4, y: 4, z: 4 (z_hi: 2, z_lo: 2; z = z_hi * 2 + z_lo), core: 2. Of those that a mesh axis runs over, the one named last changes fastest.
Arguments:
- tangents: float32 [5, 3, 32, 64, 2048], P(None, None, 'gx', None, 'gy'), may hold values from -72 to 72, as said below
- base_flow: float32 [2, 3, 32, 64, 2048], P(None, None, 'gx', None, 'gy'), may hold values from -4 to 4
- objective_weight: float32 [3, 32, 64, 2048], P(None, 'gx', None, 'gy'), may hold values from -5.6 to 5.6, as said below
Outputs:
- renormed: float32 [5, 3, 32, 64, 2048], P(None, None, 'gx', None, 'gy')
- rfactor: float32 [4, 4], replicated
- coefficients: float32 [4], replicated
- objective: float32 [5], replicated
Inputs may be any that keep to these rules, and one draw needn't show every extreme that they name: `tangents`: finite tangent velocities. `objective_weight`: finite weights.
All inputs are finite; a program needn't handle non-finite values.
Results may differ from a plain program's by a relative error of at most 0.000077.
Values sent between devices are 32-bit elements; how exact they have to be, the bound alone decides.
No kernel may reach another device: no remote copies, remote signals or barrier semaphores. Data moves between devices by JAX's collectives and lax.ppermute only.
A program may use at most 128 MiB of HBM per device.

v0:
```python
import jax
import jax.numpy as jnp
from jax import lax
from jax.sharding import PartitionSpec as P

time_step = 0.2
viscosity = 0.05


def padded_2(cells, sides, width):
    for axis, dim in sides:
        count = lax.axis_size(axis)
        head = lax.slice_in_dim(cells, 0, width, axis=dim)
        tail = lax.slice_in_dim(cells, cells.shape[dim] - width, cells.shape[dim], axis=dim)
        cells = jnp.concatenate(
            [
                lax.ppermute(tail, axis, [(i, (i + 1) % count) for i in range(count)]),
                cells,
                lax.ppermute(head, axis, [((i + 1) % count, i) for i in range(count)]),
            ],
            axis=dim,
        )
    return cells


def take_cells(values_in, step_x, step_y, step_z):
    width_x = values_in.shape[-3] - 2
    width_y = values_in.shape[-1] - 2
    if step_z != 0:
        padded = jnp.pad(values_in, [(0, 0)] * (values_in.ndim - 2) + [(1, 1), (0, 0)])
        values_in = padded[..., 1 + step_z : 1 + step_z + values_in.shape[-2], :]
    return values_in[..., 1 + step_x : 1 + step_x + width_x, :, 1 + step_y : 1 + step_y + width_y]


def gradients(values_in):
    return (
        0.5 * (take_cells(values_in, 1, 0, 0) - take_cells(values_in, -1, 0, 0)),
        0.5 * (take_cells(values_in, 0, 1, 0) - take_cells(values_in, 0, -1, 0)),
        0.5 * (take_cells(values_in, 0, 0, 1) - take_cells(values_in, 0, 0, -1)),
    )


def laplacian(values_in):
    summed = take_cells(values_in, 1, 0, 0) + take_cells(values_in, -1, 0, 0)
    summed = summed + take_cells(values_in, 0, 1, 0) + take_cells(values_in, 0, -1, 0)
    summed = summed + take_cells(values_in, 0, 0, 1) + take_cells(values_in, 0, 0, -1)
    return summed - 6.0 * take_cells(values_in, 0, 0, 0)


def rate_all(wide, flow_wide, source_mask):
    field_grad = gradients(wide)
    flow_grad = gradients(flow_wide)
    field_centre = take_cells(wide, 0, 0, 0)
    flow_centre = take_cells(flow_wide, 0, 0, 0)
    advect = (
        flow_centre[0] * field_grad[0]
        + flow_centre[1] * field_grad[1]
        + flow_centre[2] * field_grad[2]
    )
    produce = (
        field_centre[:, 0:1] * flow_grad[0]
        + field_centre[:, 1:2] * flow_grad[1]
        + field_centre[:, 2:3] * flow_grad[2]
    )
    return -advect - produce + viscosity * laplacian(wide) + source_mask * laplacian(flow_wide)


def with_rims(fields, flow_in):
    joined = jnp.concatenate([fields.reshape((15,) + fields.shape[2:]), flow_in], 0)
    padded = padded_2(joined, (("gx", 1), ("gy", 3)), 1)
    return (padded[:15].reshape((5, 3) + padded.shape[1:]), padded[15:])


def lower_inverse(lower_factor):
    count_rows = lower_factor.shape[0]
    identity_rows = jnp.eye(count_rows, dtype=lower_factor.dtype)
    inverse_rows = []
    for row_index in range(count_rows):
        row_value = identity_rows[row_index]
        for column in range(row_index):
            row_value = row_value - lower_factor[row_index, column] * inverse_rows[column]
        inverse_rows.append(row_value / lower_factor[row_index, row_index])
    return jnp.stack(inverse_rows)


def per_device(tangents, base_flow, objective_weight):
    highest = lax.Precision.HIGHEST
    local_shape = tangents.shape
    source_mask = (jnp.arange(5) == 4).astype(jnp.float32).reshape(5, 1, 1, 1, 1)
    wide, flow_wide = with_rims(tangents, base_flow[0])
    first = tangents + time_step * rate_all(wide, flow_wide, source_mask)
    wide, flow_wide = with_rims(first, base_flow[1])
    second_rate = rate_all(wide, flow_wide, source_mask)
    second = 0.5 * (tangents + first + time_step * second_rate)
    first_local = jnp.sum(objective_weight[None] * first, axis=(1, 2, 3, 4))
    second_local = jnp.sum(objective_weight[None] * second, axis=(1, 2, 3, 4))
    matrix = second.reshape(5, -1)
    gram_local = jnp.dot(matrix, matrix.T, precision=highest)
    total_cells = (
        local_shape[2] * local_shape[3] * local_shape[4] * lax.axis_size("gx") * lax.axis_size("gy")
    )
    first_total = lax.psum(first_local, ("gx", "gy"))
    gram_total, carried_total = lax.psum((gram_local, second_local), ("gx", "gy"))
    objective = 0.5 * (first_total + carried_total) / total_cells
    gram_matrix = gram_total / (3.0 * total_cells)
    lower_factor = jnp.linalg.cholesky(gram_matrix[:4, :4])
    inverse = lower_inverse(lower_factor)
    coefficients = jnp.dot(inverse, gram_matrix[:4, 4], precision=highest)
    ortho = jnp.dot(inverse, matrix[:4], precision=highest)
    last_row = matrix[4] - jnp.dot(coefficients, ortho, precision=highest)
    renormed = jnp.concatenate([ortho, last_row[None]], 0).reshape(local_shape)
    return (renormed, lower_factor.T, coefficients, objective)


def solution(mesh):
    placed = (
        P(None, None, "gx", None, "gy"),
        P(None, None, "gx", None, "gy"),
        P(None, "gx", None, "gy"),
    )
    return jax.shard_map(
        per_device,
        mesh=mesh,
        in_specs=placed,
        out_specs=(P(None, None, "gx", None, "gy"), P(), P(), P()),
        check_vma=False,
    )
```

profile of v0, /device:TPU:1, one launch (start us, length us, event | category | flops | bytes accessed | tf_op | source)
XLA Modules:
  0.0 235.3 jit_solution(13409901271503922823)
XLA Ops:
  0.6 1.2 slice_bitcast_fusion.7
  1.8 1.4 pad_maximum_fusion.8
  3.3 4.7 %collective-permute-start.1 = (f32[18,1,64,128]{3,2,1,0:T(8,128)S(1)}, f32[18,1,64,128]{3,2,1,0:T(8,128)S(1)}, u32[]{:S(2)}, u32[]{:S(2)}) collective-permute-start(f32[18,1,64,128]{3,2,1,0:T(8,128)S(1)} %get-tuple-element.57), channel_id=1, source_target_pairs={{16,0},{32,16},{48,32},{64,48},{80,64},{96,80},{112,96},{0,112},{1... | collective-permute-start | bytes 1769480 | tf_op jit(solution)/shard_map/ppermute | solution.py:19
  8.0 0.9 multiply_bitcast_fusion.2
  8.9 22.6 %collective-permute-done.1 = f32[18,1,64,128]{3,2,1,0:T(8,128)S(1)} collective-permute-done((f32[18,1,64,128]{3,2,1,0:T(8,128)S(1)}, f32[18,1,64,128]{3,2,1,0:T(8,128)S(1)}, u32[]{:S(2)}, u32[]{:S(2)}) %collective-permute-start.1) | collective-permute-done | bytes 589856 | tf_op jit(solution)/shard_map/ppermute | solution.py:19
  31.5 0.9 collective-permute-done
  32.4 0.8 copy-done.8
  33.2 0.3 pad_maximum_fusion.2
  33.5 4.1 %fusion.32 = (f32[18,6,64,1]{3,2,1,0:T(8,128)}, f32[18,6,64,1]{3,2,1,0:T(8,128)}) fusion(f32[18,6,64,128]{3,2,1,0:T(8,128)S(1)} %pad_maximum_fusion.2), kind=kLoop, calls=%fused_computation.119 | loop fusion | bytes 110592 | tf_op jit(solution)/shard_map/slice | solution.py:14
  37.6 3.0 %copy.69 = f32[18,6,64,1]{2,1,3,0:T(8,128)S(1)} copy(f32[18,6,64,1]{3,2,1,0:T(8,128)} %get-tuple-element.53) | data formatting | bytes 55296
  40.6 0.6 collective-permute-start.3
  41.2 3.6 %copy.68 = f32[18,6,64,1]{2,1,3,0:T(8,128)} copy(f32[18,6,64,1]{3,2,1,0:T(8,128)} %get-tuple-element.52) | data formatting | bytes 55296
  44.8 1.3 collective-permute-start.2
  46.1 3.2 %copy.52 = f32[18,6,64,1]{3,2,1,0:T(8,128)} copy(f32[18,6,64,1]{2,1,3,0:T(8,128)} %collective-permute-done.3) | data formatting | bytes 55296 | tf_op jit(solution)/shard_map/ppermute | solution.py:19
  49.2 2.3 collective-permute-done.2
  51.6 3.2 %copy.51 = f32[18,6,64,1]{3,2,1,0:T(8,128)} copy(f32[18,6,64,1]{2,1,3,0:T(8,128)} %collective-permute-done.2) | data formatting | bytes 55296 | tf_op jit(solution)/shard_map/ppermute | solution.py:17
  54.8 7.0 %pad_maximum_fusion = f32[18,6,64,130]{3,2,1,0:T(8,128)S(1)} fusion(f32[18,6,64,1]{3,2,1,0:T(8,128)} %copy.52, f32[18,1,64,128]{3,2,1,0:T(8,128)S(1)} %collective-permute-done.1, f32[3,4,64,128]{3,2,1,0:T(8,128)S(1)} %get-tuple-element.68, f32[15,4,64,128]{3,2,1,0:T(8,128)S(1)} %bitcast.73, f32[18,1,64,128]{3,2,1,0:T(8,128)} %copy-done.8, f32[18,6,64,1]{3,2,1,0:T(8,128)} %copy.51), kind=kLoop, calls=%fused_computation | loop fusion | flops 4492800 | bytes 7188480 | tf_op jit(solution)/shard_map/concatenate | solution.py:15
  61.8 0.7 slice.409
  62.6 0.6 slice_bitcast_fusion.5
  63.1 0.7 copy-done.5
  63.9 1.3 copy-done.3
  65.2 0.6 select_maximum_fusion.5
  65.9 0.5 subtract_multiply_fusion.5
  66.4 0.6 copy-done.11
  67.0 0.3 subtract_multiply_fusion.3
  67.4 3.8 %multiply_reduce_fusion.1 = (f32[5]{0:T(128)S(1)}, f32[5,3,4,64,128]{4,3,2,1,0:T(8,128)S(1)}) fusion(f32[3,4,64,128]{3,2,1,0:T(8,128)S(1)} %copy-done.14, f32[5,3,4,64,128]{4,3,2,1,0:T(8,128)S(1)} %copy-done, f32[3,4,64,128]{3,2,1,0:T(8,128)S(1)} %get-tuple-element.61, f32[5]{0:T(128)S(1)} %compare_convert_fusion, f32[5,3,6,64,130]{4,3,2,1,0:T(8,128)S(1)} %bitcast.84, ...), kind=kLoop, calls=%fused_computation.28 | loop fusion | flops 14745595 | bytes 23986708 | tf_op jit(solution)/shard_map/reduce_sum | solution.py:95
  71.4 2.0 collective-permute-start.5
  73.4 0.8 broadcast_multiply_fusion.1
  74.2 21.3 %collective-permute-done.5 = f32[18,1,64,128]{3,2,1,0:T(8,128)S(1)} collective-permute-done((f32[18,1,64,128]{3,2,1,0:T(8,128)S(1)}, f32[18,1,64,128]{3,2,1,0:T(8,128)S(1)}, u32[]{:S(2)}, u32[]{:S(2)}) %collective-permute-start.5) | collective-permute-done | bytes 589856 | tf_op jit(solution)/shard_map/ppermute | solution.py:19
  95.5 2.9 %collective-permute-done.4 = f32[18,1,64,128]{3,2,1,0:T(8,128)S(1)} collective-permute-done((f32[18,1,64,128]{3,2,1,0:T(8,128)S(1)}, f32[18,1,64,128]{3,2,1,0:T(8,128)S(1)}, u32[]{:S(2)}, u32[]{:S(2)}) %collective-permute-start.4) | collective-permute-done | bytes 589856 | tf_op jit(solution)/shard_map/ppermute | solution.py:17
  98.4 0.4 pad_maximum_fusion.3
  98.8 4.1 %fusion.31 = (f32[18,6,64,1]{3,2,1,0:T(8,128)}, f32[18,6,64,1]{3,2,1,0:T(8,128)}) fusion(f32[18,6,64,128]{3,2,1,0:T(8,128)S(1)} %pad_maximum_fusion.3), kind=kLoop, calls=%fused_computation.118 | loop fusion | bytes 110592 | tf_op jit(solution)/shard_map/slice | solution.py:14
  102.9 3.6 %copy.71 = f32[18,6,64,1]{2,1,3,0:T(8,128)} copy(f32[18,6,64,1]{3,2,1,0:T(8,128)} %get-tuple-element.48) | data formatting | bytes 55296
  106.5 1.6 collective-permute-start.7
  108.1 3.6 %copy.70 = f32[18,6,64,1]{2,1,3,0:T(8,128)} copy(f32[18,6,64,1]{3,2,1,0:T(8,128)} %get-tuple-element.47) | data formatting | bytes 55296
  111.9 3.2 %copy.58 = f32[18,6,64,1]{3,2,1,0:T(8,128)} copy(f32[18,6,64,1]{2,1,3,0:T(8,128)} %collective-permute-done.7) | data formatting | bytes 55296 | tf_op jit(solution)/shard_map/ppermute | solution.py:19
  115.0 2.5 %collective-permute-done.6 = f32[18,6,64,1]{2,1,3,0:T(8,128)} collective-permute-done((f32[18,6,64,1]{2,1,3,0:T(8,128)}, f32[18,6,64,1]{2,1,3,0:T(8,128)}, u32[]{:S(2)}, u32[]{:S(2)}) %collective-permute-start.6) | collective-permute-done | bytes 27680 | tf_op jit(solution)/shard_map/ppermute | solution.py:17
  117.6 3.2 %copy.57 = f32[18,6,64,1]{3,2,1,0:T(8,128)} copy(f32[18,6,64,1]{2,1,3,0:T(8,128)} %collective-permute-done.6) | data formatting | bytes 55296 | tf_op jit(solution)/shard_map/ppermute | solution.py:17
  120.8 7.2 %pad_maximum_fusion.1 = f32[18,6,64,130]{3,2,1,0:T(8,128)S(1)} fusion(f32[18,6,64,1]{3,2,1,0:T(8,128)} %copy.58, f32[18,1,64,128]{3,2,1,0:T(8,128)S(1)} %collective-permute-done.5, f32[3,4,64,128]{3,2,1,0:T(8,128)S(1)} %get-tuple-element.69, f32[15,4,64,128]{3,2,1,0:T(8,128)} %bitcast.78, f32[18,1,64,128]{3,2,1,0:T(8,128)S(1)} %collective-permute-done.4, ...), kind=kLoop, calls=%fused_computation.1 | loop fusion | flops 4492800 | bytes 7188480 | tf_op jit(solution)/shard_map/concatenate | solution.py:15
  128.0 0.4 slice.422
  128.5 0.6 slice_bitcast_fusion.2
  129.0 1.0 copy-done.4
  130.0 1.1 copy-done.6
  131.1 0.7 copy-done.2
  131.8 0.6 select_maximum_fusion
  132.4 1.2 subtract_multiply_fusion.2
  133.6 0.3 subtract_multiply_fusion
  133.9 0.6 copy-done.13
  134.7 4.7 %multiply_reduce_fusion = (f32[5]{0:T(128)S(1)}, f32[5,3,4,64,128]{4,3,2,1,0:T(8,128)S(1)}) fusion(f32[3,4,64,128]{3,2,1,0:T(8,128)S(1)} %copy-done.15, f32[3,4,64,128]{3,2,1,0:T(8,128)S(1)} %get-tuple-element.59, f32[5]{0:T(128)S(1)} %compare_convert_fusion, f32[5,3,6,64,130]{4,3,2,1,0:T(8,128)S(1)} %bitcast.82, ...), kind=kLoop, calls=%fused_computation.27 | loop fusion | flops 15237115 | bytes 25952788 | tf_op jit(solution)/shard_map/reduce_sum | solution.py:96
  139.5 0.2 broadcast_multiply_fusion
  139.6 6.8 %fusion.18 = f32[5,5]{0,1:T(8,128)S(1)} fusion(f32[5,3,4,64,128]{4,3,2,1,0:T(8,128)S(1)} %broadcast_multiply_fusion), kind=kOutput, calls=%fused_computation.43 | convolution fusion | flops 29491200 | bytes 1966180 | tf_op jit(solution)/shard_map/dot_general | solution.py:98
  146.6 68.4 %all-reduce.4 = (f32[5,5]{0,1:T(8,128)S(1)}, f32[5]{0:T(128)S(1)}) all-reduce(f32[5,5]{0,1:T(8,128)S(1)} %fusion.18, f32[5]{0:T(128)S(1)} %add.167), channel_id=1, replica_groups=mesh['gx'=8,'gy'=16] {'gx','gy'}, use_global_device_ids=true, to_apply=%region_0.1 | all-reduce | flops 30 | bytes 240 | tf_op jit(solution)/shard_map/psum | solution.py:103
  215.1 0.4 cholesky.14
  215.5 0.6 compare_reduce_fusion
  216.2 0.6 select_select_fusion
  216.8 0.7 fusion.35
  217.5 0.7 fusion.33
  218.2 6.3 %subtract_divide_fusion = (f32[1,4]{1,0:T(1,128)S(1)}, f32[1,4]{1,0:T(1,128)S(1)}, f32[1,4]{1,0:T(1,128)S(1)}, f32[1,4]{1,0:T(1,128)S(1)}) fusion(f32[4,4]{1,0:T(4,128)S(1)} %fusion.22, f32[]{:T(128)} %bitcast.29, f32[]{:T(128)} %bitcast.28, f32[]{:T(128)} %bitcast.27, f32[]{:T(128)} %bitcast.26, f32[]{:T(128)} %bitcast.25, f32[]{:T(128)} %bitcast.24, ...), kind=kLoop, calls=%fused_computation.109 | loop fusion | flops 64 | bytes 168 | tf_op jit(solution)/shard_map/div | solution.py:82
  224.6 3.5 %fusion.14 = f32[4,98304]{1,0:T(4,128)S(1)} fusion(f32[1,4,768,128]{3,2,1,0:T(8,128)S(1)} %bitcast.87, f32[1,4]{1,0:T(1,128)S(1)} %get-tuple-element.18, f32[1,4]{1,0:T(1,128)S(1)} %get-tuple-element.19, f32[1,4]{1,0:T(1,128)S(1)} %get-tuple-element.20, f32[1,4]{1,0:T(1,128)S(1)} %get-tuple-element.21), kind=kOutput, calls=%fused_computation.29 | convolution fusion | flops 18874416 | bytes 3145792 | tf_op jit(solution)/shard_map/dot_general | solution.py:109
  228.1 3.4 %fusion.23 = f32[1,98304]{1,0:T(1,128)} fusion(f32[4,98304]{1,0:T(4,128)S(1)} %fusion.14, f32[1,4]{1,0:T(1,128)S(1)} %fusion.25), kind=kOutput, calls=%fused_computation.107 | convolution fusion | flops 4718592 | bytes 1966096 | tf_op jit(solution)/shard_map/dot_general | solution.py:110
  231.7 0.7 copy.65
  232.3 0.5 broadcast_multiply_fusion.3
  232.9 1.0 sub.109
  233.9 1.4 pad_maximum_fusion.4
  (53 shorter events, 1.3 us)
Async XLA Ops:
  1.8 6.2 %copy-start.10 = (f32[2,3,4,64,128]{4,3,2,1,0:T(8,128)S(1)}, f32[2,3,4,64,128]{4,3,2,1,0:T(8,128)}, u32[]{:S(2)}) copy-start(f32[2,3,4,64,128]{4,3,2,1,0:T(8,128)} %param.4) | copy-start | bytes 2359300
  1.8 31.4 %copy-start = (f32[5,3,4,64,128]{4,3,2,1,0:T(8,128)S(1)}, f32[5,3,4,64,128]{4,3,2,1,0:T(8,128)}, u32[]{:S(2)}) copy-start(f32[5,3,4,64,128]{4,3,2,1,0:T(8,128)} %param.3) | copy-start | bytes 5898244
  3.3 28.2 %collective-permute-start.1 = (f32[18,1,64,128]{3,2,1,0:T(8,128)S(1)}, f32[18,1,64,128]{3,2,1,0:T(8,128)S(1)}, u32[]{:S(2)}, u32[]{:S(2)}) collective-permute-start(f32[18,1,64,128]{3,2,1,0:T(8,128)S(1)} %get-tuple-element.57), channel_id=1, source_target_pairs={{16,0},{32,16},{48,32},{64,48},{80,64},{96,80},{112,96},{0,112},{1... | collective-permute-start | bytes 1769480 | tf_op jit(solution)/shard_map/ppermute | solution.py:19
  8.0 24.4 %collective-permute-start = (f32[18,1,64,128]{3,2,1,0:T(8,128)S(1)}, f32[18,1,64,128]{3,2,1,0:T(8,128)S(1)}, u32[]{:S(2)}, u32[]{:S(2)}) collective-permute-start(f32[18,1,64,128]{3,2,1,0:T(8,128)S(1)} %get-tuple-element.56), channel_id=1, source_target_pairs={{0,16},{16,32},{32,48},{48,64},{64,80},{80,96},{96,112},{112,0},{1... | collective-permute-start | bytes 1769480 | tf_op jit(solution)/shard_map/ppermute | solution.py:17
  32.4 0.8 copy-start.8
  40.6 5.4 %collective-permute-start.3 = (f32[18,6,64,1]{2,1,3,0:T(8,128)S(1)}, f32[18,6,64,1]{2,1,3,0:T(8,128)}, u32[]{:S(2)}, u32[]{:S(2)}) collective-permute-start(f32[18,6,64,1]{2,1,3,0:T(8,128)S(1)} %copy.69), channel_id=1, source_target_pairs={{1,0},{2,1},{3,2},{4,3},{5,4},{6,5},{7,6},{8,7},{9,8},{10,9},{11,1... | collective-permute-start | bytes 82952 | tf_op jit(solution)/shard_map/ppermute | solution.py:19
  44.8 6.8 %collective-permute-start.2 = (f32[18,6,64,1]{2,1,3,0:T(8,128)}, f32[18,6,64,1]{2,1,3,0:T(8,128)}, u32[]{:S(2)}, u32[]{:S(2)}) collective-permute-start(f32[18,6,64,1]{2,1,3,0:T(8,128)} %copy.68), channel_id=1, source_target_pairs={{0,1},{1,2},{2,3},{3,4},{4,5},{5,6},{6,7},{7,8},{8,9},{9,10},{10,1... | collective-permute-start | bytes 82952 | tf_op jit(solution)/shard_map/ppermute | solution.py:17
  61.8 2.0 copy-start.5
  61.8 2.1 copy-start.9
  62.6 2.7 %copy-start.3 = (f32[18,6,64,1]{3,2,1,0:T(8,128)S(1)}, f32[18,6,64,1]{3,2,1,0:T(8,128)}, u32[]{:S(2)}) copy-start(f32[18,6,64,1]{3,2,1,0:T(8,128)} %copy.52) | copy-start | bytes 82948
  65.8 1.1 copy-start.11
  66.3 1.1 copy-start.14
  66.3 1.1 copy-start.18
  66.3 1.1 copy-start.19
  71.3 27.1 %copy-start.1 = (f32[5,3,4,64,128]{4,3,2,1,0:T(8,128)}, f32[5,3,4,64,128]{4,3,2,1,0:T(8,128)S(1)}, u32[]{:S(2)}) copy-start(f32[5,3,4,64,128]{4,3,2,1,0:T(8,128)S(1)} %get-tuple-element.25) | copy-start | bytes 5898244
  71.4 24.1 %collective-permute-start.5 = (f32[18,1,64,128]{3,2,1,0:T(8,128)S(1)}, f32[18,1,64,128]{3,2,1,0:T(8,128)S(1)}, u32[]{:S(2)}, u32[]{:S(2)}) collective-permute-start(f32[18,1,64,128]{3,2,1,0:T(8,128)S(1)} %get-tuple-element.55), channel_id=1, source_target_pairs={{16,0},{32,16},{48,32},{64,48},{80,64},{96,80},{112,96},{0,112},{1... | collective-permute-start | bytes 1769480 | tf_op jit(solution)/shard_map/ppermute | solution.py:19
  73.4 25.0 %collective-permute-start.4 = (f32[18,1,64,128]{3,2,1,0:T(8,128)S(1)}, f32[18,1,64,128]{3,2,1,0:T(8,128)S(1)}, u32[]{:S(2)}, u32[]{:S(2)}) collective-permute-start(f32[18,1,64,128]{3,2,1,0:T(8,128)S(1)} %get-tuple-element.54), channel_id=1, source_target_pairs={{0,16},{16,32},{32,48},{48,64},{64,80},{80,96},{96,112},{112,0},{1... | collective-permute-start | bytes 1769480 | tf_op jit(solution)/shard_map/ppermute | solution.py:17
  106.5 5.4 %collective-permute-start.7 = (f32[18,6,64,1]{2,1,3,0:T(8,128)}, f32[18,6,64,1]{2,1,3,0:T(8,128)}, u32[]{:S(2)}, u32[]{:S(2)}) collective-permute-start(f32[18,6,64,1]{2,1,3,0:T(8,128)} %copy.71), channel_id=1, source_target_pairs={{1,0},{2,1},{3,2},{4,3},{5,4},{6,5},{7,6},{8,7},{9,8},{10,9},{11,1... | collective-permute-start | bytes 82952 | tf_op jit(solution)/shard_map/ppermute | solution.py:19
  111.7 5.9 %collective-permute-start.6 = (f32[18,6,64,1]{2,1,3,0:T(8,128)}, f32[18,6,64,1]{2,1,3,0:T(8,128)}, u32[]{:S(2)}, u32[]{:S(2)}) collective-permute-start(f32[18,6,64,1]{2,1,3,0:T(8,128)} %copy.70), channel_id=1, source_target_pairs={{0,1},{1,2},{2,3},{3,4},{4,5},{5,6},{6,7},{7,8},{8,9},{9,10},{10,1... | collective-permute-start | bytes 82952 | tf_op jit(solution)/shard_map/ppermute | solution.py:17
  128.0 2.0 copy-start.4
  128.0 3.1 %copy-start.6 = (f32[18,6,64,1]{3,2,1,0:T(8,128)S(1)}, f32[18,6,64,1]{3,2,1,0:T(8,128)}, u32[]{:S(2)}) copy-start(f32[18,6,64,1]{3,2,1,0:T(8,128)} %copy.57) | copy-start | bytes 82948
  128.5 3.3 %copy-start.2 = (f32[5,3,4,64,128]{4,3,2,1,0:T(8,128)S(1)}, f32[5,3,4,64,128]{4,3,2,1,0:T(8,128)}, u32[]{:S(2)}) copy-start(f32[5,3,4,64,128]{4,3,2,1,0:T(8,128)} %copy-done.1) | copy-start | bytes 5898244
  132.3 1.2 copy-start.12
  133.6 1.0 copy-start.13
  133.6 1.1 copy-start.15
  133.6 1.1 copy-start.16
  133.6 1.2 copy-start.17
  139.6 6.8 %copy-start.7 = (f32[5,3,4,64,128]{4,3,2,1,0:T(8,128)}, f32[5,3,4,64,128]{4,3,2,1,0:T(8,128)S(1)}, u32[]{:S(2)}) copy-start(f32[5,3,4,64,128]{4,3,2,1,0:T(8,128)S(1)} %broadcast_multiply_fusion) | copy-start | bytes 5898244
  224.6 7.0 %copy-start.20 = (f32[1,4]{1,0:T(1,128)}, f32[1,4]{1,0:T(1,128)S(1)}, u32[]{:S(2)}) copy-start(f32[1,4]{1,0:T(1,128)S(1)} %fusion.25) | copy-start | bytes 52
  231.6 1.3 slice-start
where the time goes:
time: 236 us; the launch traced here: 235 us
  blocking collectives  68.4 us (29%)
  waiting for transfers between devices  52.6 us (22%)
  local copies, waits for them, and re-layouts  47.2 us (20%)
  other arithmetic  42 us (18%)
  matrix products  13.9 us (6%)
  starting transfers between devices  10.3 us (4%)
    psum x1, blocking collectives, per_device(): lax.psum((gram_local, second_local), ('gx', 'gy'))  68.4 us
    ppermute x4, waiting for transfers between devices, padded_2(): lax.ppermute(head, axis, [((i + 1) % count, i) for i in range(count)])  43.9 us
    unnamed x48, local copies, waits for them, and re-layouts  21.9 us
    concatenate x4, other arithmetic, padded_2(): jnp.concatenate([lax.ppermute(tail, axis, [(i, (i + 1) % count) for i in...  14.9 us
    ppermute x4, starting transfers between devices, padded_2(): lax.ppermute(head, axis, [((i + 1) % count, i) for i in range(count)])  8.91 us
    ppermute x4, waiting for transfers between devices, padded_2(): lax.ppermute(tail, axis, [(i, (i + 1) % count) for i in range(count)])  8.67 us
    slice x2, local copies, waits for them, and re-layouts, padded_2(): lax.slice_in_dim(cells, cells.shape[dim] - width, cells.shape[dim], axis=...  8.16 us
    dot_general x1, matrix products, per_device(): gram_local = jnp.dot(matrix, matrix.T, precision=highest)  6.8 us
  transfers between devices with their start and end apart: 8, of which 6 were waited for; matrix products, arithmetic and copies ran while one was open for 6% of the time, Pallas kernels for 0%

commit v1 on v0

--- a/solution.py
+++ b/solution.py
@@ -100,7 +100,8 @@
         local_shape[2] * local_shape[3] * local_shape[4] * lax.axis_size("gx") * lax.axis_size("gy")
     )
     first_total = lax.psum(first_local, ("gx", "gy"))
-    gram_total, carried_total = lax.psum((gram_local, second_local), ("gx", "gy"))
+    _attach_masks = lambda x_part: lax.psum(lax.psum(x_part, axis_name="gx"), axis_name="gy")
+    gram_total, carried_total = _attach_masks((gram_local, second_local))
     objective = 0.5 * (first_total + carried_total) / total_cells
     gram_matrix = gram_total / (3.0 * total_cells)
     lower_factor = jnp.linalg.cholesky(gram_matrix[:4, :4])

time: 236 us -> 287 us (1.22)
  blocking collectives: 68.4 us -> 122 us
    psum x1 -> x3, blocking collectives: 68.4 us -> 122 us  [the longest x1 70.3 us: per_device(): first_total = lax.psum(first_local, ('gx', 'gy'))]
    unnamed x48 -> x50, local copies, waits for them, and re-layouts: 21.9 us -> 21.9 us
  transfers between devices with their start and end apart: 8 -> 8, of which waited for: 6 -> 5; matrix products, arithmetic and copies ran while one was open for 6% -> 5% of each run, Pallas kernels for 0% -> 0%
where the time goes in v1:
time: 287 us; the launch traced here: 286 us
  blocking collectives  122 us (43%)
  waiting for transfers between devices  50.1 us (17%)
  local copies, waits for them, and re-layouts  47.3 us (16%)
  other arithmetic  42.1 us (15%)
  matrix products  13.9 us (5%)
  starting transfers between devices  10.3 us (4%)
    psum x1, blocking collectives, per_device(): first_total = lax.psum(first_local, ('gx', 'gy'))  70.3 us
    ppermute x4, waiting for transfers between devices, padded_2(): lax.ppermute(head, axis, [((i + 1) % count, i) for i in range(count)])  43.9 us
    psum x1, blocking collectives, per_device(): lax.psum(lax.psum(x_part, axis_name='gx'), axis_name='gy')  37.3 us
    unnamed x50, local copies, waits for them, and re-layouts  21.9 us
    concatenate x4, other arithmetic, padded_2(): jnp.concatenate([lax.ppermute(tail, axis, [(i, (i + 1) % count) for i in...  14.9 us
    psum x1, blocking collectives, per_device(): lax.psum(x_part, axis_name='gx')  13.9 us
    ppermute x4, starting transfers between devices, padded_2(): lax.ppermute(head, axis, [((i + 1) % count, i) for i in range(count)])  8.91 us
    slice x2, local copies, waits for them, and re-layouts, padded_2(): lax.slice_in_dim(cells, cells.shape[dim] - width, cells.shape[dim], axis=...  8.13 us
  transfers between devices with their start and end apart: 8, of which 5 were waited for; matrix products, arithmetic and copies ran while one was open for 5% of the time, Pallas kernels for 0%

profile of v1, /device:TPU:1, one launch (start us, length us, event | category | flops | bytes accessed | tf_op | source)
XLA Modules:
  0.0 286.2 jit_solution(10850259613232999388)
XLA Ops:
  0.6 1.2 slice_bitcast_fusion.7
  1.8 1.4 pad_maximum_fusion.8
  3.3 4.7 %collective-permute-start.1 = (f32[18,1,64,128]{3,2,1,0:T(8,128)S(1)}, f32[18,1,64,128]{3,2,1,0:T(8,128)S(1)}, u32[]{:S(2)}, u32[]{:S(2)}) collective-permute-start(f32[18,1,64,128]{3,2,1,0:T(8,128)S(1)} %get-tuple-element.59), channel_id=1, source_target_pairs={{16,0},{32,16},{48,32},{64,48},{80,64},{96,80},{112,96},{0,112},{1... | collective-permute-start | bytes 1769480 | tf_op jit(solution)/shard_map/ppermute | solution.py:19
  8.0 0.9 multiply_bitcast_fusion.2
  8.9 22.6 %collective-permute-done.1 = f32[18,1,64,128]{3,2,1,0:T(8,128)S(1)} collective-permute-done((f32[18,1,64,128]{3,2,1,0:T(8,128)S(1)}, f32[18,1,64,128]{3,2,1,0:T(8,128)S(1)}, u32[]{:S(2)}, u32[]{:S(2)}) %collective-permute-start.1) | collective-permute-done | bytes 589856 | tf_op jit(solution)/shard_map/ppermute | solution.py:19
  31.5 0.9 collective-permute-done
  32.4 0.8 copy-done.8
  33.2 0.3 pad_maximum_fusion.2
  33.5 4.1 %fusion.32 = (f32[18,6,64,1]{3,2,1,0:T(8,128)}, f32[18,6,64,1]{3,2,1,0:T(8,128)}) fusion(f32[18,6,64,128]{3,2,1,0:T(8,128)S(1)} %pad_maximum_fusion.2), kind=kLoop, calls=%fused_computation.119 | loop fusion | bytes 110592 | tf_op jit(solution)/shard_map/slice | solution.py:14
  37.6 3.0 %copy.69 = f32[18,6,64,1]{2,1,3,0:T(8,128)S(1)} copy(f32[18,6,64,1]{3,2,1,0:T(8,128)} %get-tuple-element.55) | data formatting | bytes 55296
  40.6 0.6 collective-permute-start.3
  41.2 3.6 %copy.68 = f32[18,6,64,1]{2,1,3,0:T(8,128)} copy(f32[18,6,64,1]{3,2,1,0:T(8,128)} %get-tuple-element.54) | data formatting | bytes 55296
  44.8 1.3 collective-permute-start.2
  46.0 3.2 %copy.52 = f32[18,6,64,1]{3,2,1,0:T(8,128)} copy(f32[18,6,64,1]{2,1,3,0:T(8,128)} %collective-permute-done.3) | data formatting | bytes 55296 | tf_op jit(solution)/shard_map/ppermute | solution.py:19
  49.2 2.3 collective-permute-done.2
  51.5 3.2 %copy.51 = f32[18,6,64,1]{3,2,1,0:T(8,128)} copy(f32[18,6,64,1]{2,1,3,0:T(8,128)} %collective-permute-done.2) | data formatting | bytes 55296 | tf_op jit(solution)/shard_map/ppermute | solution.py:17
  54.7 7.0 %pad_maximum_fusion = f32[18,6,64,130]{3,2,1,0:T(8,128)S(1)} fusion(f32[18,6,64,1]{3,2,1,0:T(8,128)} %copy.52, f32[18,1,64,128]{3,2,1,0:T(8,128)S(1)} %collective-permute-done.1, f32[3,4,64,128]{3,2,1,0:T(8,128)S(1)} %get-tuple-element.70, f32[15,4,64,128]{3,2,1,0:T(8,128)S(1)} %bitcast.73, f32[18,1,64,128]{3,2,1,0:T(8,128)} %copy-done.8, f32[18,6,64,1]{3,2,1,0:T(8,128)} %copy.51), kind=kLoop, calls=%fused_computation | loop fusion | flops 4492800 | bytes 7188480 | tf_op jit(solution)/shard_map/concatenate | solution.py:15
  61.8 0.7 slice.409
  62.5 0.6 slice_bitcast_fusion.5
  63.1 0.7 copy-done.5
  63.9 1.3 copy-done.3
  65.2 0.6 select_maximum_fusion.5
  65.8 0.5 subtract_multiply_fusion.5
  66.3 0.6 copy-done.11
  67.0 0.3 subtract_multiply_fusion.3
  67.4 3.8 %multiply_reduce_fusion.1 = (f32[5]{0:T(128)S(1)}, f32[5,3,4,64,128]{4,3,2,1,0:T(8,128)S(1)}) fusion(f32[3,4,64,128]{3,2,1,0:T(8,128)S(1)} %copy-done.14, f32[5,3,4,64,128]{4,3,2,1,0:T(8,128)S(1)} %copy-done, f32[3,4,64,128]{3,2,1,0:T(8,128)S(1)} %get-tuple-element.63, f32[5]{0:T(128)S(1)} %compare_convert_fusion, f32[5,3,6,64,130]{4,3,2,1,0:T(8,128)S(1)} %bitcast.84, ...), kind=kLoop, calls=%fused_computation.28 | loop fusion | flops 14745595 | bytes 23986708 | tf_op jit(solution)/shard_map/reduce_sum | solution.py:95
  71.4 2.0 collective-permute-start.5
  73.4 0.8 broadcast_multiply_fusion.1
  74.2 21.3 %collective-permute-done.5 = f32[18,1,64,128]{3,2,1,0:T(8,128)S(1)} collective-permute-done((f32[18,1,64,128]{3,2,1,0:T(8,128)S(1)}, f32[18,1,64,128]{3,2,1,0:T(8,128)S(1)}, u32[]{:S(2)}, u32[]{:S(2)}) %collective-permute-start.5) | collective-permute-done | bytes 589856 | tf_op jit(solution)/shard_map/ppermute | solution.py:19
  95.5 2.9 %collective-permute-done.4 = f32[18,1,64,128]{3,2,1,0:T(8,128)S(1)} collective-permute-done((f32[18,1,64,128]{3,2,1,0:T(8,128)S(1)}, f32[18,1,64,128]{3,2,1,0:T(8,128)S(1)}, u32[]{:S(2)}, u32[]{:S(2)}) %collective-permute-start.4) | collective-permute-done | bytes 589856 | tf_op jit(solution)/shard_map/ppermute | solution.py:17
  98.4 0.4 pad_maximum_fusion.3
  98.8 4.1 %fusion.31 = (f32[18,6,64,1]{3,2,1,0:T(8,128)}, f32[18,6,64,1]{3,2,1,0:T(8,128)}) fusion(f32[18,6,64,128]{3,2,1,0:T(8,128)S(1)} %pad_maximum_fusion.3), kind=kLoop, calls=%fused_computation.118 | loop fusion | bytes 110592 | tf_op jit(solution)/shard_map/slice | solution.py:14
  102.8 3.6 %copy.71 = f32[18,6,64,1]{2,1,3,0:T(8,128)} copy(f32[18,6,64,1]{3,2,1,0:T(8,128)} %get-tuple-element.50) | data formatting | bytes 55296
  106.4 1.6 collective-permute-start.7
  108.0 3.6 %copy.70 = f32[18,6,64,1]{2,1,3,0:T(8,128)} copy(f32[18,6,64,1]{3,2,1,0:T(8,128)} %get-tuple-element.49) | data formatting | bytes 55296
  111.8 70.3 %psum.37 = f32[5]{0:T(128)} all-reduce(f32[5]{0:T(128)S(1)} %get-tuple-element.20), channel_id=1, replica_groups=mesh['gx'=8,'gy'=16] {'gx','gy'}, use_global_device_ids=true, to_apply=%region_5.6 | all-reduce | flops 5 | bytes 40 | tf_op jit(solution)/shard_map/psum | solution.py:102
  182.1 3.2 %copy.58 = f32[18,6,64,1]{3,2,1,0:T(8,128)} copy(f32[18,6,64,1]{2,1,3,0:T(8,128)} %collective-permute-done.7) | data formatting | bytes 55296 | tf_op jit(solution)/shard_map/ppermute | solution.py:19
  185.3 3.2 %copy.57 = f32[18,6,64,1]{3,2,1,0:T(8,128)} copy(f32[18,6,64,1]{2,1,3,0:T(8,128)} %collective-permute-done.6) | data formatting | bytes 55296 | tf_op jit(solution)/shard_map/ppermute | solution.py:17
  188.5 7.2 %pad_maximum_fusion.1 = f32[18,6,64,130]{3,2,1,0:T(8,128)S(1)} fusion(f32[18,6,64,1]{3,2,1,0:T(8,128)} %copy.58, f32[18,1,64,128]{3,2,1,0:T(8,128)S(1)} %collective-permute-done.5, f32[3,4,64,128]{3,2,1,0:T(8,128)S(1)} %get-tuple-element.71, f32[15,4,64,128]{3,2,1,0:T(8,128)} %bitcast.78, f32[18,1,64,128]{3,2,1,0:T(8,128)S(1)} %collective-permute-done.4, ...), kind=kLoop, calls=%fused_computation.1 | loop fusion | flops 4492800 | bytes 7188480 | tf_op jit(solution)/shard_map/concatenate | solution.py:15
  195.7 0.4 slice.422
  196.1 0.6 slice_bitcast_fusion.2
  196.7 1.0 copy-done.4
  197.7 1.1 copy-done.6
  198.8 0.7 copy-done.2
  199.4 0.6 select_maximum_fusion
  200.0 1.2 subtract_multiply_fusion.2
  201.3 0.3 subtract_multiply_fusion
  201.6 0.6 copy-done.13
  202.4 4.9 %multiply_reduce_fusion = (f32[5]{0:T(128)S(1)}, f32[5,3,4,64,128]{4,3,2,1,0:T(8,128)S(1)}) fusion(f32[3,4,64,128]{3,2,1,0:T(8,128)S(1)} %copy-done.15, f32[3,4,64,128]{3,2,1,0:T(8,128)S(1)} %get-tuple-element.61, f32[5]{0:T(128)S(1)} %compare_convert_fusion, f32[5,3,6,64,130]{4,3,2,1,0:T(8,128)S(1)} %bitcast.82, ...), kind=kLoop, calls=%fused_computation.27 | loop fusion | flops 15237115 | bytes 25952788 | tf_op jit(solution)/shard_map/reduce_sum | solution.py:96
  207.6 6.8 %fusion.18 = f32[5,5]{0,1:T(8,128)S(1)} fusion(f32[5,3,4,64,128]{4,3,2,1,0:T(8,128)S(1)} %broadcast_multiply_fusion), kind=kOutput, calls=%fused_computation.43 | convolution fusion | flops 29491200 | bytes 1966180 | tf_op jit(solution)/shard_map/dot_general | solution.py:98
  214.4 13.9 %all-reduce.5 = (f32[5,5]{0,1:T(8,128)S(1)}, f32[5]{0:T(128)S(1)}) all-reduce(f32[5,5]{0,1:T(8,128)S(1)} %fusion.18, f32[5]{0:T(128)S(1)} %get-tuple-element.26), channel_id=1, replica_groups=mesh['gx'=8,'gy'=16] {'gx'}, use_global_device_ids=true, to_apply=%region_0.1 | all-reduce | flops 30 | bytes 240 | tf_op jit(solution)/shard_map/psum | solution.py:103
  228.4 37.3 %all-reduce.4 = (f32[5,5]{0,1:T(8,128)S(1)}, f32[5]{0:T(128)S(1)}) all-reduce(f32[5,5]{0,1:T(8,128)S(1)} %get-tuple-element.18, f32[5]{0:T(128)S(1)} %get-tuple-element.19), channel_id=1, replica_groups=mesh['gx'=8,'gy'=16] {'gy'}, use_global_device_ids=true, to_apply=%region_1.2 | all-reduce | flops 30 | bytes 240 | tf_op jit(solution)/shard_map/psum | solution.py:103
  265.8 0.4 cholesky.14
  266.2 0.6 compare_reduce_fusion
  266.9 0.6 select_select_fusion
  267.5 0.7 fusion.35
  268.2 0.7 fusion.33
  268.8 6.2 %subtract_divide_fusion = (f32[1,4]{1,0:T(1,128)S(1)}, f32[1,4]{1,0:T(1,128)S(1)}, f32[1,4]{1,0:T(1,128)S(1)}, f32[1,4]{1,0:T(1,128)S(1)}) fusion(f32[4,4]{1,0:T(4,128)S(1)} %fusion.22, f32[]{:T(128)} %bitcast.29, f32[]{:T(128)} %bitcast.28, f32[]{:T(128)} %bitcast.27, f32[]{:T(128)} %bitcast.26, f32[]{:T(128)} %bitcast.25, f32[]{:T(128)} %bitcast.24, ...), kind=kLoop, calls=%fused_computation.110 | loop fusion | flops 64 | bytes 168 | tf_op jit(solution)/shard_map/div | solution.py:82
  275.2 3.5 %fusion.14 = f32[4,98304]{1,0:T(4,128)S(1)} fusion(f32[1,4,768,128]{3,2,1,0:T(8,128)S(1)} %bitcast.87, f32[1,4]{1,0:T(1,128)S(1)} %get-tuple-element.22, f32[1,4]{1,0:T(1,128)S(1)} %get-tuple-element.23, f32[1,4]{1,0:T(1,128)S(1)} %get-tuple-element.24, f32[1,4]{1,0:T(1,128)S(1)} %get-tuple-element.25), kind=kOutput, calls=%fused_computation.29 | convolution fusion | flops 18874416 | bytes 3145792 | tf_op jit(solution)/shard_map/dot_general | solution.py:110
  278.8 3.4 %fusion.23 = f32[1,98304]{1,0:T(1,128)} fusion(f32[4,98304]{1,0:T(4,128)S(1)} %fusion.14, f32[1,4]{1,0:T(1,128)S(1)} %fusion.25), kind=kOutput, calls=%fused_computation.107 | convolution fusion | flops 4718592 | bytes 1966096 | tf_op jit(solution)/shard_map/dot_general | solution.py:111
  282.3 0.7 copy.65
  283.2 1.0 sub.109
  284.3 1.4 pad_maximum_fusion.4
  285.7 0.5 add_multiply_fusion
  (56 shorter events, 1.7 us)
Async XLA Ops:
  1.8 6.2 %copy-start.10 = (f32[2,3,4,64,128]{4,3,2,1,0:T(8,128)S(1)}, f32[2,3,4,64,128]{4,3,2,1,0:T(8,128)}, u32[]{:S(2)}) copy-start(f32[2,3,4,64,128]{4,3,2,1,0:T(8,128)} %param.4) | copy-start | bytes 2359300
  1.8 31.4 %copy-start = (f32[5,3,4,64,128]{4,3,2,1,0:T(8,128)S(1)}, f32[5,3,4,64,128]{4,3,2,1,0:T(8,128)}, u32[]{:S(2)}) copy-start(f32[5,3,4,64,128]{4,3,2,1,0:T(8,128)} %param.3) | copy-start | bytes 5898244
  3.3 28.2 %collective-permute-start.1 = (f32[18,1,64,128]{3,2,1,0:T(8,128)S(1)}, f32[18,1,64,128]{3,2,1,0:T(8,128)S(1)}, u32[]{:S(2)}, u32[]{:S(2)}) collective-permute-start(f32[18,1,64,128]{3,2,1,0:T(8,128)S(1)} %get-tuple-element.59), channel_id=1, source_target_pairs={{16,0},{32,16},{48,32},{64,48},{80,64},{96,80},{112,96},{0,112},{1... | collective-permute-start | bytes 1769480 | tf_op jit(solution)/shard_map/ppermute | solution.py:19
  8.0 24.4 %collective-permute-start = (f32[18,1,64,128]{3,2,1,0:T(8,128)S(1)}, f32[18,1,64,128]{3,2,1,0:T(8,128)S(1)}, u32[]{:S(2)}, u32[]{:S(2)}) collective-permute-start(f32[18,1,64,128]{3,2,1,0:T(8,128)S(1)} %get-tuple-element.58), channel_id=1, source_target_pairs={{0,16},{16,32},{32,48},{48,64},{64,80},{80,96},{96,112},{112,0},{1... | collective-permute-start | bytes 1769480 | tf_op jit(solution)/shard_map/ppermute | solution.py:17
  32.4 0.8 copy-start.8
  40.6 5.4 %collective-permute-start.3 = (f32[18,6,64,1]{2,1,3,0:T(8,128)S(1)}, f32[18,6,64,1]{2,1,3,0:T(8,128)}, u32[]{:S(2)}, u32[]{:S(2)}) collective-permute-start(f32[18,6,64,1]{2,1,3,0:T(8,128)S(1)} %copy.69), channel_id=1, source_target_pairs={{1,0},{2,1},{3,2},{4,3},{5,4},{6,5},{7,6},{8,7},{9,8},{10,9},{11,1... | collective-permute-start | bytes 82952 | tf_op jit(solution)/shard_map/ppermute | solution.py:19
  44.8 6.8 %collective-permute-start.2 = (f32[18,6,64,1]{2,1,3,0:T(8,128)}, f32[18,6,64,1]{2,1,3,0:T(8,128)}, u32[]{:S(2)}, u32[]{:S(2)}) collective-permute-start(f32[18,6,64,1]{2,1,3,0:T(8,128)} %copy.68), channel_id=1, source_target_pairs={{0,1},{1,2},{2,3},{3,4},{4,5},{5,6},{6,7},{7,8},{8,9},{9,10},{10,1... | collective-permute-start | bytes 82952 | tf_op jit(solution)/shard_map/ppermute | solution.py:17
  61.8 2.0 copy-start.5
  61.8 2.1 copy-start.9
  62.5 2.7 copy-start.3
  65.8 1.1 copy-start.11
  66.3 1.1 copy-start.14
  66.3 1.1 copy-start.18
  66.3 1.1 copy-start.19
  71.3 27.1 %copy-start.1 = (f32[5,3,4,64,128]{4,3,2,1,0:T(8,128)}, f32[5,3,4,64,128]{4,3,2,1,0:T(8,128)S(1)}, u32[]{:S(2)}) copy-start(f32[5,3,4,64,128]{4,3,2,1,0:T(8,128)S(1)} %get-tuple-element.21) | copy-start | bytes 5898244
  71.4 24.1 %collective-permute-start.5 = (f32[18,1,64,128]{3,2,1,0:T(8,128)S(1)}, f32[18,1,64,128]{3,2,1,0:T(8,128)S(1)}, u32[]{:S(2)}, u32[]{:S(2)}) collective-permute-start(f32[18,1,64,128]{3,2,1,0:T(8,128)S(1)} %get-tuple-element.57), channel_id=1, source_target_pairs={{16,0},{32,16},{48,32},{64,48},{80,64},{96,80},{112,96},{0,112},{1... | collective-permute-start | bytes 1769480 | tf_op jit(solution)/shard_map/ppermute | solution.py:19
  73.4 25.0 %collective-permute-start.4 = (f32[18,1,64,128]{3,2,1,0:T(8,128)S(1)}, f32[18,1,64,128]{3,2,1,0:T(8,128)S(1)}, u32[]{:S(2)}, u32[]{:S(2)}) collective-permute-start(f32[18,1,64,128]{3,2,1,0:T(8,128)S(1)} %get-tuple-element.56), channel_id=1, source_target_pairs={{0,16},{16,32},{32,48},{48,64},{64,80},{80,96},{96,112},{112,0},{1... | collective-permute-start | bytes 1769480 | tf_op jit(solution)/shard_map/ppermute | solution.py:17
  106.4 75.6 %collective-permute-start.7 = (f32[18,6,64,1]{2,1,3,0:T(8,128)}, f32[18,6,64,1]{2,1,3,0:T(8,128)}, u32[]{:S(2)}, u32[]{:S(2)}) collective-permute-start(f32[18,6,64,1]{2,1,3,0:T(8,128)} %copy.71), channel_id=1, source_target_pairs={{1,0},{2,1},{3,2},{4,3},{5,4},{6,5},{7,6},{8,7},{9,8},{10,9},{11,1... | collective-permute-start | bytes 82952 | tf_op jit(solution)/shard_map/ppermute | solution.py:19
  111.6 73.6 %collective-permute-start.6 = (f32[18,6,64,1]{2,1,3,0:T(8,128)}, f32[18,6,64,1]{2,1,3,0:T(8,128)}, u32[]{:S(2)}, u32[]{:S(2)}) collective-permute-start(f32[18,6,64,1]{2,1,3,0:T(8,128)} %copy.70), channel_id=1, source_target_pairs={{0,1},{1,2},{2,3},{3,4},{4,5},{5,6},{6,7},{7,8},{8,9},{9,10},{10,1... | collective-permute-start | bytes 82952 | tf_op jit(solution)/shard_map/ppermute | solution.py:17
  195.7 2.0 copy-start.4
  195.7 3.1 %copy-start.6 = (f32[18,6,64,1]{3,2,1,0:T(8,128)S(1)}, f32[18,6,64,1]{3,2,1,0:T(8,128)}, u32[]{:S(2)}) copy-start(f32[18,6,64,1]{3,2,1,0:T(8,128)} %copy.57) | copy-start | bytes 82948
  196.1 3.3 %copy-start.2 = (f32[5,3,4,64,128]{4,3,2,1,0:T(8,128)S(1)}, f32[5,3,4,64,128]{4,3,2,1,0:T(8,128)}, u32[]{:S(2)}) copy-start(f32[5,3,4,64,128]{4,3,2,1,0:T(8,128)} %copy-done.1) | copy-start | bytes 5898244
  200.0 1.2 copy-start.12
  201.2 1.0 copy-start.13
  201.2 1.1 copy-start.15
  201.2 1.1 copy-start.16
  201.2 1.2 copy-start.17
  207.5 6.9 %copy-start.7 = (f32[5,3,4,64,128]{4,3,2,1,0:T(8,128)}, f32[5,3,4,64,128]{4,3,2,1,0:T(8,128)S(1)}, u32[]{:S(2)}) copy-start(f32[5,3,4,64,128]{4,3,2,1,0:T(8,128)S(1)} %broadcast_multiply_fusion) | copy-start | bytes 5898244
  275.2 7.0 %copy-start.20 = (f32[1,4]{1,0:T(1,128)}, f32[1,4]{1,0:T(1,128)S(1)}, u32[]{:S(2)}) copy-start(f32[1,4]{1,0:T(1,128)S(1)} %fusion.25) | copy-start | bytes 52
  282.2 1.0 slice-start
  284.3 1.4 copy-start.21
